TPU v7x, 32 devices: a whole 2x2x4 slice. The times are simulated.
32 devices in a mesh: group: 4 (over y, x), member: 8 (over z, core).
Axes of the slice: x: 2, y: 2, z: 4, core: 2. Of those that a mesh axis runs over, the one named last changes fastest.
Arguments:
- old_ids: int32 [512], P(('group', 'member')), may hold values from -1 to 255, as said below
- field_old: float32 [512, 32, 1024], P(('group', 'member')), may hold values from -6 to 6
- source_old: float32 [512, 32, 1024], P(('group', 'member')), may hold values from -12 to 12
- kappa_old: float32 [512, 32, 1024], P(('group', 'member')), may hold values from 0.5 to 5
- refine: int32 [256], P(('group', 'member')), may hold values 0 or 1
- neighbors: int32 [256, 6], P(('group', 'member')), may hold values from -1 to 255, as said below
- coarse_inverse: float32 [4, 512, 512], P('group', 'member'), may hold values from -0.0546875 to 0.0546875
Outputs:
- solution: float32 [256, 32, 1024], P(('group', 'member'))
Inputs may be any that keep to these rules, and one draw needn't show every extreme that they name: `old_ids`: on each device the live slots come first and hold consecutive curve indices in increasing order, devices following one another along the curve; every block's new owner (index // 8) is the device that holds it or the next one; some device fills all 16 slots. Blocks form a grid in Morton order (bit i of a curve index is a bit of coordinate i mod 3); neighbors[g, k] is either -1 or the block adjacent to g across face k in that grid; relations are mutual: neighbors[g, k] = h means neighbors[h, k xor 1] = g.
All inputs are finite; a program needn't handle non-finite values. No bound on the sum of `refine` on one device may be relied on, other than what follows from the above.
Results may differ from a plain program's by a relative error of at most 0.000078.
Values sent between devices are 32-bit elements; how exact they have to be, the bound alone decides.
A program may use at most 128 MiB of HBM per device.

v0:
```python
import functools

import jax
import jax.numpy as jnp
from jax import lax
from jax.experimental import pallas as pl
from jax.experimental.pallas import tpu as pltpu
from jax.sharding import PartitionSpec as P

OMEGA = 0.8
AXES = ("group", "member")
NB, EDGE, FACE = 8, 32, 1024
HIGHEST = lax.Precision.HIGHEST
VMEM_LIMIT = 40 * 2**20
VM = pl.BlockSpec(memory_space=pltpu.VMEM)
SM = pl.BlockSpec(memory_space=pltpu.SMEM)
FACE_SHAPES = ((4, FACE), (EDGE, 128), (8, FACE))


def roll(value, steps):
    width = value.shape[-1]
    return pltpu.roll(value, steps % width, value.ndim - 1)


def depth_lanes(shape):
    return lax.broadcasted_iota(jnp.int32, shape, len(shape) - 1) % EDGE


def blocks_of(axis, side):
    return [b for b in range(NB) if (b >> axis) % 2 == side]


def pack_faces(load, outs):
    segment = lax.broadcasted_iota(jnp.int32, (EDGE, 128), 1) // EDGE
    depth = depth_lanes((8, FACE))
    everything = slice(0, FACE)
    for side in (0, 1):
        for j, b in enumerate(blocks_of(0, side)):
            row = (EDGE - 1) * side
            outs[0][side][j : j + 1, :] = load(b, slice(row, row + 1), everything)
        packed = jnp.zeros((EDGE, 128), jnp.float32)
        for j, b in enumerate(blocks_of(1, side)):
            low = (FACE - 128) * side
            piece = load(b, slice(0, EDGE), slice(low, low + 128))
            packed = jnp.where(segment == j, roll(piece, EDGE * (j - 3 * side)), packed)
        outs[1][side][...] = packed
        packed = jnp.zeros((8, FACE), jnp.float32)
        for j, b in enumerate(blocks_of(2, side)):
            for part in range(4):
                slot = 4 * j + part
                piece = load(b, slice(8 * part, 8 * part + 8), everything)
                packed = jnp.where(depth == slot, roll(piece, slot - 31 * side), packed)
        outs[2][side][...] = packed


def fill(values, ghosts, nbrs, pad, sheet, mirror):
    everything = slice(0, FACE)
    depth = depth_lanes((8, FACE))
    for b in range(NB):
        pad[b, 8:40, 128 : 128 + FACE] = values[b]
        for side in (0, 1):
            inside = [(b >> axis) % 2 != side for axis in range(3)]
            has = [nbrs[b, 2 * axis + side] >= 0 for axis in range(3)]
            j = [blocks_of(a, side).index(b) if not inside[a] else 0 for a in range(3)]
            row, far = (EDGE - 1) * side, (EDGE - 1) * (1 - side)
            if inside[0]:
                ghost = values[b ^ 1, far : far + 1, :]
            else:
                ghost = ghosts[0][side][j[0] : j[0] + 1, :]
            spare = values[b, row : row + 1, :] if mirror else jnp.zeros_like(ghost)
            place = 7 + 33 * side
            pad[b, place : place + 1, 128 : 128 + FACE] = jnp.where(has[0], ghost, spare)
            low, high = (FACE - 128) * side, (FACE - 128) * (1 - side)
            if inside[1]:
                ghost = values[b ^ 2, :, high : high + 128]
            else:
                ghost = roll(ghosts[1][side][...], EDGE * (3 * (1 - side) - j[1]))
            if mirror:
                spare = roll(values[b, :, low : low + 128], EDGE * (3 - 6 * side))
            else:
                spare = jnp.zeros_like(ghost)
            place = (128 + FACE) * side
            pad[b, 8:40, place : place + 128] = jnp.where(has[1], ghost, spare)
        for part in range(4):
            rows = slice(8 * part, 8 * part + 8)
            own = values[b, rows, :]
            near = []
            for side in (0, 1):
                if (b >> 2) % 2 != side:
                    ghost = roll(values[b ^ 4, rows, :], 31 * (2 * side - 1))
                else:
                    slot = 4 * blocks_of(2, side).index(b) + part
                    ghost = roll(ghosts[2][side][...], 31 * side - slot)
                spare = own if mirror else jnp.zeros_like(own)
                near.append(jnp.where(nbrs[b, 4 + side] >= 0, ghost, spare))
            sheet[b, rows, :] = jnp.where(depth < EDGE // 2, near[0], near[1])


def across(pad, sheet, b, part):
    depth = depth_lanes((8, FACE))
    top = 8 + 8 * part
    inner = slice(128, 128 + FACE)
    x_minus = pad[b, top - 1 : top + 7, inner]
    x_plus = pad[b, top + 1 : top + 9, inner]
    whole = pad[b, top : top + 8, :]
    edge = sheet[b, 8 * part : 8 * part + 8, :]
    y_minus = roll(whole, EDGE)[:, inner]
    y_plus = roll(whole, -EDGE)[:, inner]
    z_minus = jnp.where(depth == 0, edge, roll(whole, 1)[:, inner])
    z_plus = jnp.where(depth == EDGE - 1, edge, roll(whole, -1)[:, inner])
    return whole[:, inner], (x_minus, x_plus, y_minus, y_plus, z_minus, z_plus)


def terms(pad_u, sheet_u, pad_k, sheet_k, b, part, half_scale):
    u, around_u = across(pad_u, sheet_u, b, part)
    k, around_k = across(pad_k, sheet_k, b, part)
    applied = jnp.zeros_like(u)
    diagonal = jnp.zeros_like(u)
    for other_u, other_k in zip(around_u, around_k):
        weight = k + other_k
        applied = applied + weight * (u - other_u)
        diagonal = diagonal + weight
    return u, half_scale * applied, half_scale * diagonal


def pairs(refs):
    return [refs[2 * axis : 2 * axis + 2] for axis in range(3)]


def merge_kernel(moved, *refs):
    mine, theirs, merged = refs[0:3], refs[3:6], refs[6:9]
    out_u, out_k = pairs(refs[9:15]), pairs(refs[15:21])
    count = moved[0]

    def body(p, carry):
        for own, got, out in zip(mine, theirs, merged):
            out[p] = jnp.where(p < count, got[p], own[jnp.maximum(p - count, 0)])
        return carry

    lax.fori_loop(0, NB, body, 0)
    for values, outs in ((merged[0], out_u), (merged[2], out_k)):
        pack_faces(lambda b, rows, lanes, values=values: values[b, rows, lanes], outs)


def smooth_kernel(last, nbrs, refine, u_ref, f_ref, k_ref, *refs):
    ghosts_u, ghosts_k = pairs(refs[0:6]), pairs(refs[6:12])
    outs = refs[12:-4]
    pad_u, sheet_u, pad_k, sheet_k = refs[-4:]
    fill(u_ref, ghosts_u, nbrs, pad_u, sheet_u, False)
    fill(k_ref, ghosts_k, nbrs, pad_k, sheet_k, True)

    def body(b, carry):
        half_scale = 0.5 + 0.5 * refine[b].astype(jnp.float32)
        total = None
        for part in range(4):
            rows = slice(8 * part, 8 * part + 8)
            u, applied, diagonal = terms(pad_u, sheet_u, pad_k, sheet_k, b, part, half_scale)
            gap = f_ref[b, rows, :] - applied
            if not last:
                outs[0][b, rows, :] = u + OMEGA * gap / diagonal
            else:
                total = gap if part % 2 == 0 else total + gap
                if part % 2 == 1:
                    outs[0][b, part // 2] = total
        return carry

    lax.fori_loop(0, NB, body, 0)
    if not last:
        pack_faces(lambda b, rows, lanes: outs[0][b, rows, lanes], pairs(outs[1:7]))


def finish_kernel(u_ref, rows_ref, out_ref):
    for b in range(NB):
        for part in range(4):
            place = 2 * b + part // 2
            rows = slice(8 * part, 8 * part + 8)
            out_ref[b, rows, :] = u_ref[b, rows, :] + rows_ref[place : place + 1, :]


def face_partners(members, devices):
    here = lax.axis_index("group") * members + lax.axis_index("member")
    nbits = devices.bit_length() - 1
    bits = [here // 2**i % 2 for i in range(nbits)]
    result = []
    for axis in range(3):
        own = [i for i in range(nbits) if i % 3 == axis]
        extent = 2 ** len(own)
        coord = sum(bits[i] * 2**n for n, i in enumerate(own))
        base = here - sum(bits[i] * 2**i for i in own)
        pair = []
        for step in (-1, 1):
            moved = coord + step
            inside = jnp.logical_and(moved >= 0, moved < extent)
            clipped = jnp.clip(moved, 0, extent - 1)
            index = base + sum(clipped // 2**n % 2 * 2**i for n, i in enumerate(own))
            pair.append((inside, (index // members, index % members)))
        result.append(pair)
    return result


def exchange_kernel(members, devices, sets, *refs):
    count = 6 * sets
    sources, targets = refs[:count], refs[count : 2 * count]
    send, recv = refs[2 * count :]
    partners = face_partners(members, devices)
    barrier = pltpu.get_barrier_semaphore()
    present = jnp.int32(0)
    for axis in range(3):
        for side in (0, 1):
            inside, peer = partners[axis][side]
            present = present + inside.astype(jnp.int32)

            @pl.when(inside)
            def _():
                pl.semaphore_signal(
                    barrier, inc=1, device_id=peer, device_id_type=pl.DeviceIdType.MESH
                )

    pl.semaphore_wait(barrier, present)

    def copy_of(group, axis, side, peer):
        out = 6 * group + 2 * axis + side
        into = 6 * group + 2 * axis + 1 - side
        return pltpu.make_async_remote_copy(
            src_ref=sources[out],
            dst_ref=targets[into],
            send_sem=send.at[out],
            recv_sem=recv.at[into],
            device_id=peer,
            device_id_type=pl.DeviceIdType.MESH,
        )

    every = [(g, a, s) for g in range(sets) for a in range(3) for s in (0, 1)]
    for group, axis, side in every:
        inside, peer = partners[axis][side]

        @pl.when(inside)
        def _():
            copy_of(group, axis, side, peer).start()

    for group, axis, side in every:
        inside, peer = partners[axis][side]

        @pl.when(inside)
        def _():
            copy_of(group, axis, side, peer).wait_send()
            copy_of(group, axis, 1 - side, peer).wait_recv()


def exchange(faces, ident):
    sets = len(faces) // 6
    shapes = [jax.ShapeDtypeStruct(f.shape, f.dtype) for f in faces]
    members = lax.axis_size("member")
    devices = lax.axis_size(AXES)
    return pl.pallas_call(
        functools.partial(exchange_kernel, members, devices, sets),
        out_shape=shapes,
        in_specs=[VM] * len(faces),
        out_specs=[VM] * len(faces),
        scratch_shapes=[
            pltpu.SemaphoreType.DMA((len(faces),)),
            pltpu.SemaphoreType.DMA((len(faces),)),
        ],
        compiler_params=pltpu.CompilerParams(collective_id=ident, has_side_effects=True),
    )(*faces)


def gather_kernel(members, mine, out, send, recv, local_sem):
    me = lax.axis_index("member")
    barrier = pltpu.get_barrier_semaphore()
    for step in range(1, members):
        pl.semaphore_signal(
            barrier,
            inc=1,
            device_id={"member": (me + step) % members},
            device_id_type=pl.DeviceIdType.MESH,
        )
    pl.semaphore_wait(barrier, members - 1)

    def copy_of(step):
        return pltpu.make_async_remote_copy(
            src_ref=mine,
            dst_ref=out.at[me],
            send_sem=send.at[step],
            recv_sem=recv.at[step],
            device_id={"member": (me + step) % members},
            device_id_type=pl.DeviceIdType.MESH,
        )

    for step in range(1, members):
        copy_of(step).start()
    out[me] = mine[...]
    for step in range(1, members):
        copy_of(step).wait_send()
        copy_of(step).wait_recv()


def gather(rows, ident):
    members = lax.axis_size("member")
    return pl.pallas_call(
        functools.partial(gather_kernel, members),
        out_shape=jax.ShapeDtypeStruct((members,) + rows.shape, rows.dtype),
        in_specs=[VM],
        out_specs=VM,
        scratch_shapes=[
            pltpu.SemaphoreType.DMA((members,)),
            pltpu.SemaphoreType.DMA((members,)),
            pltpu.SemaphoreType.DMA,
        ],
        compiler_params=pltpu.CompilerParams(collective_id=ident, has_side_effects=True),
    )(rows)


def face_structs():
    return [jax.ShapeDtypeStruct(s, jnp.float32) for s in FACE_SHAPES for _ in (0, 1)]


def smooth(last, nbrs, refine, u, f, k, ghosts_u, ghosts_k):
    if last:
        outs = [jax.ShapeDtypeStruct((NB, 2, 8, FACE), jnp.float32)]
    else:
        outs = [jax.ShapeDtypeStruct(u.shape, jnp.float32)] + face_structs()
    return pl.pallas_call(
        functools.partial(smooth_kernel, last),
        out_shape=outs,
        in_specs=[SM, SM] + [VM] * 15,
        out_specs=[VM] * len(outs),
        scratch_shapes=[
            pltpu.VMEM((NB, 48, FACE + 256), jnp.float32),
            pltpu.VMEM((NB, EDGE, FACE), jnp.float32),
            pltpu.VMEM((NB, 48, FACE + 256), jnp.float32),
            pltpu.VMEM((NB, EDGE, FACE), jnp.float32),
        ],
        compiler_params=pltpu.CompilerParams(vmem_limit_bytes=VMEM_LIMIT),
    )(nbrs, refine, u, f, k, *ghosts_u, *ghosts_k)


def local(old_ids, field_old, source_old, kappa_old, refine, neighbors, coarse_inverse):
    devices = lax.axis_size(AXES)
    here = lax.axis_index(AXES)
    kept = jnp.sum(
        jnp.logical_and(old_ids >= 0, old_ids // NB == here).astype(jnp.int32), dtype=jnp.int32
    )
    olds = (field_old, source_old, kappa_old)
    leaving = [lax.dynamic_slice_in_dim(a, kept, NB, 0) for a in olds]
    arrived = lax.ppermute(leaving, AXES, [(i, i + 1) for i in range(devices - 1)])
    block = pl.BlockSpec((NB, EDGE, FACE), lambda i: (0, 0, 0))
    whole = jax.ShapeDtypeStruct((NB, EDGE, FACE), jnp.float32)
    small = [pl.BlockSpec(s, lambda i: (0, 0)) for s in FACE_SHAPES for _ in (0, 1)]
    merged = pl.pallas_call(
        merge_kernel,
        grid=(1,),
        out_shape=[whole] * 3 + face_structs() * 2,
        in_specs=[SM] + [block] * 6,
        out_specs=[block] * 3 + small * 2,
        compiler_params=pltpu.CompilerParams(vmem_limit_bytes=VMEM_LIMIT),
    )((NB - kept)[None], *olds, *arrived)
    u, f, k = merged[:3]
    ghosts = exchange(merged[3:], 1)
    ghosts_u, ghosts_k = ghosts[:6], ghosts[6:]
    for sweep in range(2):
        u, *faces = smooth(False, neighbors, refine, u, f, k, ghosts_u, ghosts_k)
        ghosts_u = exchange(faces, 2 + sweep)
    (sums,) = smooth(True, neighbors, refine, u, f, k, ghosts_u, ghosts_k)
    lanes = lax.iota(jnp.int32, FACE)
    cell = lanes // (FACE // 2) * 2 + lanes % EDGE // (EDGE // 2)
    choose = (cell[:, None] == lax.iota(jnp.int32, 128)[None, :]).astype(jnp.float32)
    rows = jnp.sum(sums, axis=2).reshape(2 * NB, FACE)
    coarse = jnp.dot(rows, choose, precision=HIGHEST) * (EDGE // 2) ** (-1.5)
    gathered = gather(coarse, 4)[:, :, :4].reshape(-1)
    e = jnp.dot(coarse_inverse[0], gathered, precision=HIGHEST)
    lifted = jnp.broadcast_to(
        e.reshape(2 * NB, 2, 1, 2, 1), (2 * NB, 2, EDGE // 2, 2, EDGE // 2)
    ).reshape(2 * NB, FACE)
    return pl.pallas_call(
        finish_kernel,
        out_shape=whole,
        in_specs=[VM, VM],
        out_specs=VM,
        compiler_params=pltpu.CompilerParams(vmem_limit_bytes=VMEM_LIMIT),
    )(u, lifted)


def solution(mesh):
    in_specs = (
        P(AXES),
        P(AXES, None, None),
        P(AXES, None, None),
        P(AXES, None, None),
        P(AXES),
        P(AXES, None),
        P("group", "member", None),
    )
    return jax.shard_map(
        local, mesh=mesh, in_specs=in_specs, out_specs=P(AXES, None, None), check_vma=False
    )
```

profile of v0, /device:TPU:0, one launch (start us, length us, event | category | flops | bytes accessed | tf_op | source)
XLA Modules:
  0.0 146.5 jit_solution(4303533127727299052)
XLA Ops:
  0.0 1.4 fusion.19
  3.1 2.5 %constant_dynamic-slice_fusion.2 = f32[8,32,1024]{2,1,0:T(8,128)} fusion(f32[16,32,1024]{2,1,0:T(8,128)} %refs_0_.1, s32[]{:T(128)S(6)} %select_n.38), kind=kLoop, calls=%fused_computation.37 | loop fusion | bytes 2097156 | tf_op jit(solution)/shard_map/dynamic_slice | solution.py:345
  5.6 2.5 %collective-permute-start = (f32[8,32,1024]{2,1,0:T(8,128)}, f32[8,32,1024]{2,1,0:T(8,128)S(1)}, u32[]{:S(2)}, u32[]{:S(2)}) collective-permute-start(f32[8,32,1024]{2,1,0:T(8,128)} %constant_dynamic-slice_fusion.2), channel_id=1, source_target_pairs={{0,1},{1,2},{2,3},{3,4},{4,5},{5,6},{6,7},{7,8},{8,9},{9,10},{10,1... | collective-permute-start | bytes 3145736 | tf_op jit(solution)/shard_map/ppermute | solution.py:346
  8.2 1.1 constant_dynamic-slice_fusion.1
  9.3 4.6 %collective-permute-start.1 = (f32[8,32,1024]{2,1,0:T(8,128)}, f32[8,32,1024]{2,1,0:T(8,128)S(1)}, u32[]{:S(2)}, u32[]{:S(2)}) collective-permute-start(f32[8,32,1024]{2,1,0:T(8,128)} %constant_dynamic-slice_fusion.1), channel_id=1, source_target_pairs={{0,1},{1,2},{2,3},{3,4},{4,5},{5,6},{6,7},{7,8},{8,9},{9,10},{10,1... | collective-permute-start | bytes 3145736 | tf_op jit(solution)/shard_map/ppermute | solution.py:346
  13.9 1.1 constant_dynamic-slice_fusion
  15.0 1.9 %collective-permute-start.2 = (f32[8,32,1024]{2,1,0:T(8,128)}, f32[8,32,1024]{2,1,0:T(8,128)S(1)}, u32[]{:S(2)}, u32[]{:S(2)}) collective-permute-start(f32[8,32,1024]{2,1,0:T(8,128)} %constant_dynamic-slice_fusion), channel_id=1, source_target_pairs={{0,1},{1,2},{2,3},{3,4},{4,5},{5,6},{6,7},{7,8},{8,9},{9,10},{10,1... | collective-permute-start | bytes 3145736 | tf_op jit(solution)/shard_map/ppermute | solution.py:346
  20.3 1.6 %copy-done = f32[16,32,1024]{2,1,0:T(8,128)S(1)} copy-done((f32[16,32,1024]{2,1,0:T(8,128)S(1)}, f32[16,32,1024]{2,1,0:T(8,128)}, u32[]{:S(2)}) %copy-start) | copy-done | bytes 2097176
  21.9 1.6 %copy-done.2 = f32[16,32,1024]{2,1,0:T(8,128)S(1)} copy-done((f32[16,32,1024]{2,1,0:T(8,128)S(1)}, f32[16,32,1024]{2,1,0:T(8,128)}, u32[]{:S(2)}) %copy-start.2) | copy-done | bytes 2097176
  23.5 1.6 %copy-done.4 = f32[16,32,1024]{2,1,0:T(8,128)S(1)} copy-done((f32[16,32,1024]{2,1,0:T(8,128)S(1)}, f32[16,32,1024]{2,1,0:T(8,128)}, u32[]{:S(2)}) %copy-start.4) | copy-done | bytes 2097176
  25.1 1.2 copy-done.9
  26.3 1.2 copy-done.11
  27.5 1.0 shard_map.73
  36.8 37.2 %shard_map.74 = (f32[4,1024]{1,0:T(4,128)}, f32[4,1024]{1,0:T(4,128)}, f32[32,128]{1,0:T(8,128)}, f32[32,128]{1,0:T(8,128)}, f32[8,1024]{1,0:T(8,128)}, /*index=...) custom-call(f32[4,1024]{1,0:T(4,128)} %copy-done.53, ...), custom_call_target="tpu_custom_call" | custom-call | tf_op jit(solution)/shard_map/pallas_call | solution.py:255
  74.0 1.2 copy-done.7
  84.0 5.5 %shard_map.75 = (f32[8,32,1024]{2,1,0:T(8,128)S(1)}, f32[4,1024]{1,0:T(4,128)S(1)}, f32[4,1024]{1,0:T(4,128)S(1)}, f32[32,128]{1,0:T(8,128)S(1)}, f32[32,128]{1,...) custom-call(s32[8,6]{1,0:T(8,128)S(1)} %copy-done.26, s32[8]{0:T(128)S(1)} %copy-done.69, ...), custom_call_target="tpu_custom_call" | custom-call | tf_op jit(solution)/shard_map/pallas_call | solution.py:323
  94.1 6.9 %shard_map.76 = (f32[4,1024]{1,0:T(4,128)}, f32[4,1024]{1,0:T(4,128)}, f32[32,128]{1,0:T(8,128)}, f32[32,128]{1,0:T(8,128)}, f32[8,1024]{1,0:T(8,128)}, /*index=5*/f32[8,1024]{1,0:T(8,128)}) custom-call(f32[4,1024]{1,0:T(4,128)} %copy-done.61, f32[4,1024]{1,0:T(4,128)} %copy-done.62, f32[32,128]{1,0:T(8,128)} %copy-done.63, f32[32,128]{1,0:T(8,128)} %copy-done.64, ...), custom_call_target="tpu_custom_call" | custom-call | tf_op jit(solution)/shard_map/pallas_call | solution.py:255
  101.0 1.2 copy-done.13
  106.6 5.5 %shard_map.77 = (f32[8,32,1024]{2,1,0:T(8,128)S(1)}, f32[4,1024]{1,0:T(4,128)S(1)}, f32[4,1024]{1,0:T(4,128)S(1)}, f32[32,128]{1,0:T(8,128)S(1)}, f32[32,128]{1,...) custom-call(s32[8,6]{1,0:T(8,128)S(1)} %copy-done.26, s32[8]{0:T(128)S(1)} %copy-done.69, ...), custom_call_target="tpu_custom_call" | custom-call | tf_op jit(solution)/shard_map/pallas_call | solution.py:323
  115.8 6.6 %shard_map.78 = (f32[4,1024]{1,0:T(4,128)}, f32[4,1024]{1,0:T(4,128)}, f32[32,128]{1,0:T(8,128)}, f32[32,128]{1,0:T(8,128)}, f32[8,1024]{1,0:T(8,128)}, /*index=5*/f32[8,1024]{1,0:T(8,128)}) custom-call(f32[4,1024]{1,0:T(4,128)} %copy-done.65, f32[4,1024]{1,0:T(4,128)} %copy-done.66, f32[32,128]{1,0:T(8,128)} %copy-done.67, f32[32,128]{1,0:T(8,128)} %copy-done.68, ...), custom_call_target="tpu_custom_call" | custom-call | tf_op jit(solution)/shard_map/pallas_call | solution.py:255
  126.7 5.2 %shard_map.79 = f32[8,2,8,1024]{3,2,1,0:T(8,128)S(1)} custom-call(s32[8,6]{1,0:T(8,128)S(1)} %copy-done.26, s32[8]{0:T(128)S(1)} %copy-done.69, f32[8,32,1024]{2,1,0:T(8,128)S(1)} %get-tuple-element.98.u_ref, f32[8,32,1024]{2,1,0:T(8,128)S(1)} %get-tuple-element.59.f_ref, f32[8,32,1024]{2,1,0:T(8,128)S(1)} %get-tuple-element.60.k_ref, ...), custom_call_target="tpu_custom_call" | custom-call | tf_op jit(solution)/shard_map/pallas_call | solution.py:323
  132.7 1.2 reduce_sum.19
  135.0 7.9 %shard_map.80 = f32[8,16,128]{2,1,0:T(8,128)} custom-call(f32[16,128]{1,0:T(8,128)} %convolution_multiply_fusion.mine), custom_call_target="tpu_custom_call" | custom-call | tf_op jit(solution)/shard_map/pallas_call | solution.py:300
  145.5 1.1 shard_map.81
  (147 shorter events, 41.2 us)
Async XLA Ops:
  0.0 8.1 %copy-start.1 = (f32[16,32,1024]{2,1,0:T(8,128)S(1)}, f32[16,32,1024]{2,1,0:T(8,128)}, u32[]{:S(2)}) copy-start(f32[16,32,1024]{2,1,0:T(8,128)} %refs_1_.1) | copy-start | bytes 6291460
  3.1 10.7 %copy-start.3 = (f32[16,32,1024]{2,1,0:T(8,128)S(1)}, f32[16,32,1024]{2,1,0:T(8,128)}, u32[]{:S(2)}) copy-start(f32[16,32,1024]{2,1,0:T(8,128)} %refs_2_.1) | copy-start | bytes 6291460
  5.6 11.8 %copy-start.70 = (f32[1,64,512]{2,1,0:T(8,128)S(1)}, f32[1,64,512]{2,1,0:T(8,128)}, u32[]{:S(2)}) copy-start(f32[1,64,512]{2,1,0:T(8,128)} %param.13) | copy-start | bytes 393220
  5.6 12.0 %collective-permute-start = (f32[8,32,1024]{2,1,0:T(8,128)}, f32[8,32,1024]{2,1,0:T(8,128)S(1)}, u32[]{:S(2)}, u32[]{:S(2)}) collective-permute-start(f32[8,32,1024]{2,1,0:T(8,128)} %constant_dynamic-slice_fusion.2), channel_id=1, source_target_pairs={{0,1},{1,2},{2,3},{3,4},{4,5},{5,6},{6,7},{7,8},{8,9},{9,10},{10,1... | collective-permute-start | bytes 3145736 | tf_op jit(solution)/shard_map/ppermute | solution.py:346
  9.3 8.3 %collective-permute-start.1 = (f32[8,32,1024]{2,1,0:T(8,128)}, f32[8,32,1024]{2,1,0:T(8,128)S(1)}, u32[]{:S(2)}, u32[]{:S(2)}) collective-permute-start(f32[8,32,1024]{2,1,0:T(8,128)} %constant_dynamic-slice_fusion.1), channel_id=1, source_target_pairs={{0,1},{1,2},{2,3},{3,4},{4,5},{5,6},{6,7},{7,8},{8,9},{9,10},{10,1... | collective-permute-start | bytes 3145736 | tf_op jit(solution)/shard_map/ppermute | solution.py:346
  15.0 4.3 %collective-permute-start.2 = (f32[8,32,1024]{2,1,0:T(8,128)}, f32[8,32,1024]{2,1,0:T(8,128)S(1)}, u32[]{:S(2)}, u32[]{:S(2)}) collective-permute-start(f32[8,32,1024]{2,1,0:T(8,128)} %constant_dynamic-slice_fusion), channel_id=1, source_target_pairs={{0,1},{1,2},{2,3},{3,4},{4,5},{5,6},{6,7},{7,8},{8,9},{9,10},{10,1... | collective-permute-start | bytes 3145736 | tf_op jit(solution)/shard_map/ppermute | solution.py:346
  17.6 1.0 copy-start.8
  19.3 1.0 copy-start.10
  20.3 1.6 %copy-start = (f32[16,32,1024]{2,1,0:T(8,128)S(1)}, f32[16,32,1024]{2,1,0:T(8,128)}, u32[]{:S(2)}) copy-start(f32[16,32,1024]{2,1,0:T(8,128)} %refs_0_.1) | copy-start | bytes 6291460
  21.9 1.6 %copy-start.2 = (f32[16,32,1024]{2,1,0:T(8,128)S(1)}, f32[16,32,1024]{2,1,0:T(8,128)}, u32[]{:S(2)}) copy-start(f32[16,32,1024]{2,1,0:T(8,128)} %refs_1_.1) | copy-start | bytes 6291460
  23.5 1.6 %copy-start.4 = (f32[16,32,1024]{2,1,0:T(8,128)S(1)}, f32[16,32,1024]{2,1,0:T(8,128)}, u32[]{:S(2)}) copy-start(f32[16,32,1024]{2,1,0:T(8,128)} %refs_2_.1) | copy-start | bytes 6291460
  25.1 1.2 copy-start.9
  26.3 1.2 copy-start.11
  27.5 46.4 %copy-start.26 = (s32[8,6]{1,0:T(8,128)S(1)}, s32[8,6]{1,0:T(8,128)}, u32[]{:S(2)}) copy-start(s32[8,6]{1,0:T(8,128)} %nbrs.5) | copy-start | bytes 580
  27.5 46.4 %copy-start.69 = (s32[8]{0:T(128)S(1)}, s32[8]{0:T(128)}, u32[]{:S(2)}) copy-start(s32[8]{0:T(128)} %refine.5) | copy-start | bytes 100
  28.6 1.0 copy-start.6
  74.0 27.0 %copy-start.19 = (f32[4,1024]{1,0:T(4,128)S(1)}, f32[4,1024]{1,0:T(4,128)}, u32[]{:S(2)}) copy-start(f32[4,1024]{1,0:T(4,128)} %get-tuple-element.79.refs_6_) | copy-start | bytes 49156
  74.0 1.2 copy-start.7
  84.0 17.0 %copy-start.15 = (f32[8,1024]{1,0:T(8,128)S(1)}, f32[8,1024]{1,0:T(8,128)}, u32[]{:S(2)}) copy-start(f32[8,1024]{1,0:T(8,128)} %get-tuple-element.83.refs_10_) | copy-start | bytes 98308
  84.0 17.0 %copy-start.17 = (f32[8,1024]{1,0:T(8,128)S(1)}, f32[8,1024]{1,0:T(8,128)}, u32[]{:S(2)}) copy-start(f32[8,1024]{1,0:T(8,128)} %get-tuple-element.84.refs_11_) | copy-start | bytes 98308
  84.0 17.0 %copy-start.21 = (f32[4,1024]{1,0:T(4,128)S(1)}, f32[4,1024]{1,0:T(4,128)}, u32[]{:S(2)}) copy-start(f32[4,1024]{1,0:T(4,128)} %get-tuple-element.80.refs_7_) | copy-start | bytes 49156
  84.0 17.0 %copy-start.23 = (f32[32,128]{1,0:T(8,128)S(1)}, f32[32,128]{1,0:T(8,128)}, u32[]{:S(2)}) copy-start(f32[32,128]{1,0:T(8,128)} %get-tuple-element.81.refs_8_) | copy-start | bytes 49156
  84.0 17.0 %copy-start.25 = (f32[32,128]{1,0:T(8,128)S(1)}, f32[32,128]{1,0:T(8,128)}, u32[]{:S(2)}) copy-start(f32[32,128]{1,0:T(8,128)} %get-tuple-element.82.refs_9_) | copy-start | bytes 49156
  101.0 1.2 copy-start.13
  (50 other events, 33.8 us)
where the time goes:
time: 149 us; the launch traced here: 147 us
  Pallas kernels  76.7 us (51%)
  local copies, waits for them, and re-layouts  53.2 us (36%)
  starting transfers between devices  9.03 us (6%)
  other arithmetic  2.66 us (2%)
  between operations  2.62 us (2%)
  matrix products  1.56 us (1%)
    pallas_call x3, Pallas kernels, exchange(): pl.pallas_call(functools.partial(exchange_kernel, members, devices, sets)...  50.6 us
    unnamed x142, local copies, waits for them, and re-layouts  46.4 us
    pallas_call x3, Pallas kernels, smooth(): pl.pallas_call(functools.partial(smooth_kernel, last), out_shape=outs, in...  16.1 us
    ppermute x3, starting transfers between devices, local(): lax.ppermute(leaving, AXES, [(i, i + 1) for i in range(devices - 1)])  9.03 us
    pallas_call x1, Pallas kernels, gather(): pl.pallas_call(functools.partial(gather_kernel, members), out_shape=jax.S...  7.85 us
    dynamic_slice x3, local copies, waits for them, and re-layouts, local(): leaving = [lax.dynamic_slice_in_dim(a, kept, NB, 0) for a in olds]  4.67 us
  transfers between devices with their start and end apart: 3, of which 1 were waited for; matrix products, arithmetic and copies ran while one was open for 2% of the time, Pallas kernels for 0%

commit v1 on v0

v1 whole, which is shorter than its diff:
```python
import functools

import jax
import jax.numpy as jnp
from jax import lax
from jax.experimental import pallas as pl
from jax.experimental.pallas import tpu as pltpu
from jax.sharding import PartitionSpec as P

OMEGA = 0.8
AXES = ("group", "member")
NB, EDGE, FACE = 8, 32, 1024
HIGHEST = lax.Precision.HIGHEST
VMEM_LIMIT = 56 * 2**20
VM = pl.BlockSpec(memory_space=pltpu.VMEM)
ANY = pl.BlockSpec(memory_space=pl.ANY)
MESH = pl.DeviceIdType.MESH
SM = pl.BlockSpec(memory_space=pltpu.SMEM)
FACE_SHAPES = ((4, FACE), (EDGE, 128), (8, FACE))


def roll(value, steps):
    width = value.shape[-1]
    return pltpu.roll(value, steps % width, value.ndim - 1)


def depth_lanes(shape):
    return lax.broadcasted_iota(jnp.int32, shape, len(shape) - 1) % EDGE


def blocks_of(axis, side):
    return [b for b in range(NB) if (b >> axis) % 2 == side]


def pack_faces(load, outs):
    segment = lax.broadcasted_iota(jnp.int32, (EDGE, 128), 1) // EDGE
    depth = depth_lanes((8, FACE))
    everything = slice(0, FACE)
    for side in (0, 1):
        for j, b in enumerate(blocks_of(0, side)):
            row = (EDGE - 1) * side
            outs[0][side][j : j + 1, :] = load(b, slice(row, row + 1), everything)
        packed = jnp.zeros((EDGE, 128), jnp.float32)
        for j, b in enumerate(blocks_of(1, side)):
            low = (FACE - 128) * side
            piece = load(b, slice(0, EDGE), slice(low, low + 128))
            packed = jnp.where(segment == j, roll(piece, EDGE * (j - 3 * side)), packed)
        outs[1][side][...] = packed
        packed = jnp.zeros((8, FACE), jnp.float32)
        for j, b in enumerate(blocks_of(2, side)):
            for part in range(4):
                slot = 4 * j + part
                piece = load(b, slice(8 * part, 8 * part + 8), everything)
                packed = jnp.where(depth == slot, roll(piece, slot - 31 * side), packed)
        outs[2][side][...] = packed


def fill(values, ghosts, nbrs, pad, sheet, mirror):
    everything = slice(0, FACE)
    depth = depth_lanes((8, FACE))
    for b in range(NB):
        pad[b, 8:40, 128 : 128 + FACE] = values[b]
        for side in (0, 1):
            inside = [(b >> axis) % 2 != side for axis in range(3)]
            has = [nbrs[b, 2 * axis + side] >= 0 for axis in range(3)]
            j = [blocks_of(a, side).index(b) if not inside[a] else 0 for a in range(3)]
            row, far = (EDGE - 1) * side, (EDGE - 1) * (1 - side)
            if inside[0]:
                ghost = values[b ^ 1, far : far + 1, :]
            else:
                ghost = ghosts[0][side][j[0] : j[0] + 1, :]
            spare = values[b, row : row + 1, :] if mirror else jnp.zeros_like(ghost)
            place = 7 + 33 * side
            pad[b, place : place + 1, 128 : 128 + FACE] = jnp.where(has[0], ghost, spare)
            low, high = (FACE - 128) * side, (FACE - 128) * (1 - side)
            if inside[1]:
                ghost = values[b ^ 2, :, high : high + 128]
            else:
                ghost = roll(ghosts[1][side][...], EDGE * (3 * (1 - side) - j[1]))
            if mirror:
                spare = roll(values[b, :, low : low + 128], EDGE * (3 - 6 * side))
            else:
                spare = jnp.zeros_like(ghost)
            place = (128 + FACE) * side
            pad[b, 8:40, place : place + 128] = jnp.where(has[1], ghost, spare)
        for part in range(4):
            rows = slice(8 * part, 8 * part + 8)
            own = values[b, rows, :]
            near = []
            for side in (0, 1):
                if (b >> 2) % 2 != side:
                    ghost = roll(values[b ^ 4, rows, :], 31 * (2 * side - 1))
                else:
                    slot = 4 * blocks_of(2, side).index(b) + part
                    ghost = roll(ghosts[2][side][...], 31 * side - slot)
                spare = own if mirror else jnp.zeros_like(own)
                near.append(jnp.where(nbrs[b, 4 + side] >= 0, ghost, spare))
            sheet[b, rows, :] = jnp.where(depth < EDGE // 2, near[0], near[1])


def across(pad, sheet, b, part):
    depth = depth_lanes((8, FACE))
    top = 8 + 8 * part
    inner = slice(128, 128 + FACE)
    x_minus = pad[b, top - 1 : top + 7, inner]
    x_plus = pad[b, top + 1 : top + 9, inner]
    whole = pad[b, top : top + 8, :]
    edge = sheet[b, 8 * part : 8 * part + 8, :]
    y_minus = roll(whole, EDGE)[:, inner]
    y_plus = roll(whole, -EDGE)[:, inner]
    z_minus = jnp.where(depth == 0, edge, roll(whole, 1)[:, inner])
    z_plus = jnp.where(depth == EDGE - 1, edge, roll(whole, -1)[:, inner])
    return whole[:, inner], (x_minus, x_plus, y_minus, y_plus, z_minus, z_plus)


def face_partners(members, devices):
    here = lax.axis_index("group") * members + lax.axis_index("member")
    nbits = devices.bit_length() - 1
    bits = [here // 2**i % 2 for i in range(nbits)]
    result = []
    for axis in range(3):
        own = [i for i in range(nbits) if i % 3 == axis]
        extent = 2 ** len(own)
        coord = sum(bits[i] * 2**n for n, i in enumerate(own))
        base = here - sum(bits[i] * 2**i for i in own)
        pair = []
        for step in (-1, 1):
            moved = coord + step
            inside = jnp.logical_and(moved >= 0, moved < extent)
            clipped = jnp.clip(moved, 0, extent - 1)
            index = base + sum(clipped // 2**n % 2 * 2**i for n, i in enumerate(own))
            pair.append((inside, (index // members, index % members)))
        result.append(pair)
    return result


def main_kernel(
    members, devices, old_ids, nbrs, refine, inverse, u_old, f_old, k_old, out_ref, *scratch
):
    olds, stages, gots = scratch[0:3], scratch[3:6], scratch[6:9]
    u_ref, f_ref, k_ref, pad_u, sheet_u, pad_k, sheet_k, weights, sums, mine, all_sums = scratch[9:20]
    sent, ghost = [], []
    for phase in range(4):
        base = 20 + 6 * phase
        sent.append([[r.at[0], r.at[1]] for r in scratch[base : base + 3]])
        ghost.append([[r.at[0], r.at[1]] for r in scratch[base + 3 : base + 6]])
    in_sem, move_send, move_recv, face_send, face_recv, sum_send, sum_recv = scratch[44:51]

    member = lax.axis_index("member")
    here = lax.axis_index("group") * members + member
    partners = face_partners(members, devices)
    has_next, has_prev = here < devices - 1, here > 0
    after = jnp.minimum(here + 1, devices - 1)
    before = jnp.maximum(here - 1, 0)
    after = (after // members, after % members)
    before = (before // members, before % members)

    order = (0, 2, 1)
    loads = [
        pltpu.make_async_copy(ref, olds[i], in_sem.at[i])
        for i, ref in enumerate((u_old, f_old, k_old))
    ]
    for i in order:
        loads[i].start()

    barrier = pltpu.get_barrier_semaphore()
    expected = has_next.astype(jnp.int32) + (members - 1)
    for axis in range(3):
        for side in (0, 1):
            inside, peer = partners[axis][side]
            expected = expected + inside.astype(jnp.int32)

            @pl.when(inside)
            def _():
                pl.semaphore_signal(barrier, inc=1, device_id=peer, device_id_type=MESH)

    for step in range(1, members):
        pl.semaphore_signal(
            barrier,
            inc=1,
            device_id={"member": (member + step) % members},
            device_id_type=MESH,
        )

    @pl.when(has_prev)
    def _():
        pl.semaphore_signal(barrier, inc=1, device_id=before, device_id_type=MESH)

    kept = jnp.int32(0)
    for slot in range(2 * NB):
        index = old_ids[slot]
        own = jnp.logical_and(index >= here * NB, index < here * NB + NB)
        kept = kept + own.astype(jnp.int32)
    kept = jnp.minimum(kept, NB)
    count = NB - kept

    moves = [
        pltpu.make_async_remote_copy(
            src_ref=stages[i],
            dst_ref=gots[i],
            send_sem=move_send.at[i],
            recv_sem=move_recv.at[i],
            device_id=after,
            device_id_type=MESH,
        )
        for i in range(3)
    ]
    for i in order:
        loads[i].wait()

        def stage(p, carry, i=i):
            stages[i][p] = olds[i][kept + p]
            return carry

        lax.fori_loop(0, NB, stage, 0)
        if i == 0:
            pl.semaphore_wait(barrier, expected)

        @pl.when(has_next)
        def _():
            moves[i].start()

    def settle(i, out):
        @pl.when(has_prev)
        def _():
            moves[i].wait_recv()

        def body(p, carry):
            out[p] = jnp.where(p < count, gots[i][p], olds[i][jnp.maximum(p - count, 0)])
            return carry

        lax.fori_loop(0, NB, body, 0)

    def face_copy(phase, axis, side, peer):
        return pltpu.make_async_remote_copy(
            src_ref=sent[phase][axis][side],
            dst_ref=ghost[phase][axis][1 - side],
            send_sem=face_send.at[phase, 2 * axis + side],
            recv_sem=face_recv.at[phase, 2 * axis + 1 - side],
            device_id=peer,
            device_id_type=MESH,
        )

    def send_faces(phase, values):
        pack_faces(lambda b, rows, lanes: values[b, rows, lanes], sent[phase])
        for axis in range(3):
            for side in (0, 1):
                inside, peer = partners[axis][side]

                @pl.when(inside)
                def _():
                    face_copy(phase, axis, side, peer).start()

    def take_faces(phase):
        for axis in range(3):
            for side in (0, 1):
                inside, peer = partners[axis][side]

                @pl.when(inside)
                def _():
                    face_copy(phase, axis, side, peer).wait_send()
                    face_copy(phase, axis, 1 - side, peer).wait_recv()

    settle(0, u_ref)
    send_faces(0, u_ref)
    settle(2, k_ref)
    send_faces(3, k_ref)
    take_faces(0)
    fill(u_ref, ghost[0], nbrs, pad_u, sheet_u, False)
    take_faces(3)
    fill(k_ref, ghost[3], nbrs, pad_k, sheet_k, True)

    def weigh(b, carry):
        half_scale = 0.5 + 0.5 * refine[b].astype(jnp.float32)
        for part in range(4):
            rows = slice(8 * part, 8 * part + 8)
            k, around = across(pad_k, sheet_k, b, part)
            for face in range(6):
                weights[b, face, rows, :] = half_scale * (k + around[face])
        return carry

    lax.fori_loop(0, NB, weigh, 0)
    settle(1, f_ref)

    def terms(b, part, with_diagonal):
        rows = slice(8 * part, 8 * part + 8)
        u, around = across(pad_u, sheet_u, b, part)
        applied = jnp.zeros_like(u)
        diagonal = jnp.zeros_like(u)
        for face in range(6):
            weight = weights[b, face, rows, :]
            applied = applied + weight * (u - around[face])
            if with_diagonal:
                diagonal = diagonal + weight
        return u, f_ref[b, rows, :] - applied, diagonal

    def sweep(b, carry):
        for part in range(4):
            u, gap, diagonal = terms(b, part, True)
            u_ref[b, 8 * part : 8 * part + 8, :] = u + OMEGA * gap / diagonal
        return carry

    for phase in (1, 2):
        lax.fori_loop(0, NB, sweep, 0)
        send_faces(phase, u_ref)
        take_faces(phase)
        fill(u_ref, ghost[phase], nbrs, pad_u, sheet_u, False)

    def residual(b, carry):
        for half in (0, 1):
            gap = terms(b, 2 * half, False)[1] + terms(b, 2 * half + 1, False)[1]
            sums[2 * b + half] = gap
        return carry

    lax.fori_loop(0, NB, residual, 0)

    def cell_of(lane):
        return lane // (FACE // 2) * 2 + lane % EDGE // (EDGE // 2)

    choose = cell_of(lax.broadcasted_iota(jnp.int32, (FACE, 128), 0)) == lax.broadcasted_iota(
        jnp.int32, (FACE, 128), 1
    )
    rows = jnp.sum(sums[...], axis=1)
    mine[...] = jnp.dot(
        rows, choose.astype(jnp.float32), precision=HIGHEST, preferred_element_type=jnp.float32
    ) * (EDGE // 2) ** (-1.5)

    def sum_copy(step):
        return pltpu.make_async_remote_copy(
            src_ref=mine,
            dst_ref=all_sums.at[member],
            send_sem=sum_send.at[step],
            recv_sem=sum_recv.at[step],
            device_id={"member": (member + step) % members},
            device_id_type=MESH,
        )

    for step in range(1, members):
        sum_copy(step).start()
    all_sums[member] = mine[...]
    for step in range(1, members):
        sum_copy(step).wait_send()
        sum_copy(step).wait_recv()

    coarse = all_sums[...].reshape(members * 2 * NB, 128)
    lane = lax.broadcasted_iota(jnp.int32, (8 * NB, 128), 1)
    total = jnp.zeros((8 * NB, 128), jnp.float32)
    for c in range(4):
        product = jnp.dot(
            inverse[c], coarse, precision=HIGHEST, preferred_element_type=jnp.float32
        )
        total = total + jnp.where(lane == c, product, 0.0)
    column = jnp.sum(total, axis=1, keepdims=True)
    place = lax.broadcasted_iota(jnp.int32, (8 * NB, FACE), 0)
    cell = cell_of(lax.broadcasted_iota(jnp.int32, (8 * NB, FACE), 1))
    spread = jnp.where(place % 4 == cell, column, 0.0)
    rows_of = lax.broadcasted_iota(jnp.int32, (2 * NB, 8 * NB), 1) // 4
    pick = (rows_of == lax.broadcasted_iota(jnp.int32, (2 * NB, 8 * NB), 0)).astype(jnp.float32)
    lifted = jnp.dot(pick, spread, precision=HIGHEST, preferred_element_type=jnp.float32)
    for b in range(NB):
        for half in (0, 1):
            part = slice(16 * half, 16 * half + 16)
            row = 2 * b + half
            out_ref[b, part, :] = u_ref[b, part, :] + lifted[row : row + 1, :]

    @pl.when(has_next)
    def _():
        for i in order:
            moves[i].wait_send()


def local(old_ids, field_old, source_old, kappa_old, refine, neighbors, coarse_inverse):
    members = lax.axis_size("member")
    devices = lax.axis_size(AXES)
    inverse = coarse_inverse[0].reshape(8 * NB, members * 2 * NB, 4).transpose(2, 0, 1)
    whole = (NB, EDGE, FACE)
    shapes = [field_old.shape] * 3 + [whole] * 9
    padded = (NB, 48, FACE + 256)
    shapes += [padded, whole, padded, whole, (NB, 6, EDGE, FACE), (2 * NB, 8, FACE)]
    shapes += [(2 * NB, 128), (members, 2 * NB, 128)]
    shapes += [(2,) + s for _ in range(8) for s in FACE_SHAPES]
    dma = pltpu.SemaphoreType.DMA
    scratch = [pltpu.VMEM(s, jnp.float32) for s in shapes]
    scratch += [dma((3,)), dma((3,)), dma((3,)), dma((4, 6)), dma((4, 6))]
    scratch += [dma((members,)), dma((members,))]
    return pl.pallas_call(
        functools.partial(main_kernel, members, devices),
        out_shape=jax.ShapeDtypeStruct(whole, jnp.float32),
        in_specs=[SM, SM, SM, VM, ANY, ANY, ANY],
        out_specs=VM,
        scratch_shapes=scratch,
        compiler_params=pltpu.CompilerParams(
            collective_id=1, has_side_effects=True, vmem_limit_bytes=VMEM_LIMIT
        ),
    )(old_ids, neighbors, refine, inverse, field_old, source_old, kappa_old)


def solution(mesh):
    in_specs = (
        P(AXES),
        P(AXES, None, None),
        P(AXES, None, None),
        P(AXES, None, None),
        P(AXES),
        P(AXES, None),
        P("group", "member", None),
    )
    return jax.shard_map(
        local, mesh=mesh, in_specs=in_specs, out_specs=P(AXES, None, None), check_vma=False
    )
```

time: 149 us -> 74 us (0.50); the launches traced: 147 us -> 73.8 us
  local copies, waits for them, and re-layouts: 53.2 us -> 4.12 us
  starting transfers between devices: 9.03 us -> 0 us
  Pallas kernels: 76.7 us -> 69.7 us
  other arithmetic: 2.66 us -> 0 us
  between operations: 2.62 us -> 0.02 us
  matrix products: 1.56 us -> 0 us
    unnamed x142 -> x2, local copies, waits for them, and re-layouts: 46.4 us -> 3.33 us
    ppermute x3 -> x0, starting transfers between devices: 9.03 us -> none  [local(): lax.ppermute(leaving, AXES, [(i, i + 1) for i in range(devices - 1)])]
    pallas_call x9 -> x1, Pallas kernels: 76.7 us -> 69.7 us  [local(): pl.pallas_call(functools.partial(main_kernel, members, devices), out_shap...]
    dynamic_slice x3 -> x0, local copies, waits for them, and re-layouts: 4.67 us -> none  [local(): leaving = [lax.dynamic_slice_in_dim(a, kept, NB, 0) for a in olds]]
    reduce_sum x2 -> x0, other arithmetic: 2.65 us -> none  [the longest x1 1.44 us: local(): jnp.sum(jnp.logical_and(old_ids >= 0, old_ids // NB == here).astype(jnp.i...]
    reshape x3 -> x0, local copies, waits for them, and re-layouts: 1.76 us -> none  [the longest x1 0.94 us: local(): gathered = gather(coarse, 4)[:, :, :4].reshape(-1)]
    dot_general x2 -> x0, matrix products: 1.56 us -> none  [the longest x1 0.99 us: local(): coarse = jnp.dot(rows, choose, precision=HIGHEST) * (EDGE // 2) ** (-1.5)]
  transfers between devices with their start and end apart: 3 -> 0, of which waited for: 1 -> 0; matrix products, arithmetic and copies ran while one was open for 2% -> 0% of each run, Pallas kernels for 0% -> 0%
where the time goes in v1:
time: 74 us; the launch traced here: 73.8 us
  Pallas kernels  69.7 us (94%)
  local copies, waits for them, and re-layouts  4.12 us (6%)
    pallas_call x1, Pallas kernels, local(): pl.pallas_call(functools.partial(main_kernel, members, devices), out_shap...  69.7 us
    unnamed x2, local copies, waits for them, and re-layouts  3.33 us

profile of v1, /device:TPU:0, one launch (start us, length us, event | category | flops | bytes accessed | tf_op | source)
XLA Modules:
  0.0 73.8 jit_solution(8750808881437452369)
XLA Ops:
  0.0 1.0 %copy.8 = f32[1,64,512]{1,2,0:T(8,128)S(1)} copy(f32[1,64,512]{2,1,0:T(8,128)} %param.13) | data formatting | bytes 262144 | tf_op args[6]
  1.0 0.8 %copy.9 = f32[64,128,4]{1,0,2:T(8,128)} copy(f32[64,128,4]{0,2,1:T(4,128)S(1)} %bitcast.2) | data formatting | bytes 262144 | tf_op jit(solution)/shard_map/reshape;squeeze | solution.py:375
  1.8 69.7 %shard_map.73 = f32[8,32,1024]{2,1,0:T(8,128)} custom-call(s32[16]{0:T(128)} %old_ids.1, s32[8,6]{1,0:T(8,128)} %nbrs.1, s32[8]{0:T(128)} %refine.1, f32[4,64,128]{2,1,0:T(8,128)} %bitcast.3, f32[16,32,1024]{2,1,0:T(8,128)} %u_old.1, f32[16,32,1024]{2,1,0:T(8,128)} %f_old.1, f32[16,32,1024]{2,1,0:T(8,128)} %k_old.1), custom_call_target="tpu_custom_call" | custom-call | tf_op jit(solution)/shard_map/pallas_call | solution.py:386
  71.5 2.3 %copy.11 = f32[8,32,1024]{2,1,0:T(8,128)} copy(f32[8,32,1024]{2,1,0:T(8,128)} %shard_map.73) | data formatting | bytes 2097152

commit v2 on v1

--- a/solution.py
+++ b/solution.py
@@ -135,7 +135,7 @@
 
 
 def main_kernel(
-    members, devices, old_ids, nbrs, refine, inverse, u_old, f_old, k_old, out_ref, *scratch
+    members, devices, old_ids, nbrs, refine, inverse, u_old, f_old, k_old, out_ref, low_ref, high_ref, *scratch
 ):
     olds, stages, gots = scratch[0:3], scratch[3:6], scratch[6:9]
     u_ref, f_ref, k_ref, pad_u, sheet_u, pad_k, sheet_k, weights, sums, mine, all_sums = scratch[9:20]
@@ -343,25 +343,25 @@
         sum_copy(step).wait_recv()
 
     coarse = all_sums[...].reshape(members * 2 * NB, 128)
-    lane = lax.broadcasted_iota(jnp.int32, (8 * NB, 128), 1)
-    total = jnp.zeros((8 * NB, 128), jnp.float32)
-    for c in range(4):
-        product = jnp.dot(
-            inverse[c], coarse, precision=HIGHEST, preferred_element_type=jnp.float32
-        )
-        total = total + jnp.where(lane == c, product, 0.0)
-    column = jnp.sum(total, axis=1, keepdims=True)
+    cells = members * 8 * NB
+    lane = lax.broadcasted_iota(jnp.int32, (128, cells), 1) % 4
+    copies = (lane == lax.broadcasted_iota(jnp.int32, (128, cells), 0)).astype(jnp.float32)
+    repeated = jnp.dot(coarse, copies, precision=HIGHEST, preferred_element_type=jnp.float32)
+    owner = lax.broadcasted_iota(jnp.int32, repeated.shape, 1) // 4
+    chosen = owner == lax.broadcasted_iota(jnp.int32, repeated.shape, 0)
+    vector = jnp.sum(jnp.where(chosen, repeated, 0.0), axis=0, keepdims=True)
+    column = jnp.sum(inverse[0] * vector, axis=1, keepdims=True)
     place = lax.broadcasted_iota(jnp.int32, (8 * NB, FACE), 0)
     cell = cell_of(lax.broadcasted_iota(jnp.int32, (8 * NB, FACE), 1))
     spread = jnp.where(place % 4 == cell, column, 0.0)
-    rows_of = lax.broadcasted_iota(jnp.int32, (2 * NB, 8 * NB), 1) // 4
-    pick = (rows_of == lax.broadcasted_iota(jnp.int32, (2 * NB, 8 * NB), 0)).astype(jnp.float32)
-    lifted = jnp.dot(pick, spread, precision=HIGHEST, preferred_element_type=jnp.float32)
-    for b in range(NB):
-        for half in (0, 1):
-            part = slice(16 * half, 16 * half + 16)
-            row = 2 * b + half
-            out_ref[b, part, :] = u_ref[b, part, :] + lifted[row : row + 1, :]
+    rows_of = lax.broadcasted_iota(jnp.int32, (NB, 8 * NB), 1) // 4
+    for half, rows_ref in ((0, low_ref), (1, high_ref)):
+        wanted = 2 * lax.broadcasted_iota(jnp.int32, (NB, 8 * NB), 0) + half
+        pick = (rows_of == wanted).astype(jnp.float32)
+        rows_ref[...] = jnp.dot(
+            pick, spread, precision=HIGHEST, preferred_element_type=jnp.float32
+        )
+    out_ref[...] = u_ref[...]
 
     @pl.when(has_next)
     def _():
@@ -372,7 +372,6 @@
 def local(old_ids, field_old, source_old, kappa_old, refine, neighbors, coarse_inverse):
     members = lax.axis_size("member")
     devices = lax.axis_size(AXES)
-    inverse = coarse_inverse[0].reshape(8 * NB, members * 2 * NB, 4).transpose(2, 0, 1)
     whole = (NB, EDGE, FACE)
     shapes = [field_old.shape] * 3 + [whole] * 9
     padded = (NB, 48, FACE + 256)
@@ -383,16 +382,22 @@
     scratch = [pltpu.VMEM(s, jnp.float32) for s in shapes]
     scratch += [dma((3,)), dma((3,)), dma((3,)), dma((4, 6)), dma((4, 6))]
     scratch += [dma((members,)), dma((members,))]
-    return pl.pallas_call(
+    u, low, high = pl.pallas_call(
         functools.partial(main_kernel, members, devices),
-        out_shape=jax.ShapeDtypeStruct(whole, jnp.float32),
+        out_shape=[
+            jax.ShapeDtypeStruct(whole, jnp.float32),
+            jax.ShapeDtypeStruct((NB, FACE), jnp.float32),
+            jax.ShapeDtypeStruct((NB, FACE), jnp.float32),
+        ],
         in_specs=[SM, SM, SM, VM, ANY, ANY, ANY],
-        out_specs=VM,
+        out_specs=[VM, VM, VM],
         scratch_shapes=scratch,
         compiler_params=pltpu.CompilerParams(
             collective_id=1, has_side_effects=True, vmem_limit_bytes=VMEM_LIMIT
         ),
-    )(old_ids, neighbors, refine, inverse, field_old, source_old, kappa_old)
+    )(old_ids, neighbors, refine, coarse_inverse, field_old, source_old, kappa_old)
+    half = lax.broadcasted_iota(jnp.int32, (1, EDGE, 1), 1) < EDGE // 2
+    return u + jnp.where(half, low[:, None, :], high[:, None, :])
 
 
 def solution(mesh):

time: 74 us -> 72.5 us (0.980)
  local copies, waits for them, and re-layouts: 4.12 us -> 0 us
  other arithmetic: 0 us -> 2.46 us
    unnamed x2 -> x0, local copies, waits for them, and re-layouts: 3.33 us -> none
    add x0 -> x1, other arithmetic: none -> 2.46 us  [local(): return u + jnp.where(half, low[:, None, :], high[:, None, :])]
    another operation x1 -> x0, local copies, waits for them, and re-layouts: 0.78 us -> none  [local(): coarse_inverse[0].reshape(8 * NB, members * 2 * NB, 4).transpose(2, 0, 1)]
where the time goes in v2:
time: 72.5 us; the launch traced here: 72.3 us
  Pallas kernels  69.8 us (96%)
  other arithmetic  2.46 us (3%)
    pallas_call x1, Pallas kernels, local(): pl.pallas_call(functools.partial(main_kernel, members, devices), out_shap...  69.8 us
    add x1, other arithmetic, local(): return u + jnp.where(half, low[:, None, :], high[:, None, :])  2.46 us

profile of v2, /device:TPU:0, one launch (start us, length us, event | category | flops | bytes accessed | tf_op | source)
XLA Modules:
  0.0 72.3 jit_solution(2292947379046126262)
XLA Ops:
  0.0 69.8 %shard_map.73 = (f32[8,32,1024]{2,1,0:T(8,128)}, f32[8,1024]{1,0:T(8,128)}, f32[8,1024]{1,0:T(8,128)}) custom-call(s32[16]{0:T(128)} %old_ids.1, s32[8,6]{1,0:T(8,128)} %nbrs.1, s32[8]{0:T(128)} %refine.1, f32[1,64,512]{2,1,0:T(8,128)} %inverse.1, f32[16,32,1024]{2,1,0:T(8,128)} %u_old.1, f32[16,32,1024]{2,1,0:T(8,128)} %f_old.1, f32[16,32,1024]{2,1,0:T(8,128)} %k_old.1), custom_call_target="tpu_custom_call" | custom-call | tf_op jit(solution)/shard_map/pallas_call | solution.py:385
  69.9 2.5 %select_add_fusion = f32[8,32,1024]{2,1,0:T(8,128)} fusion(f32[8,32,1024]{2,1,0:T(8,128)} %get-tuple-element.8, f32[8,1024]{1,0:T(8,128)} %get-tuple-element.10, f32[8,1024]{1,0:T(8,128)} %get-tuple-element.9, pred[32]{0:T(512)(128)(4,1)S(1)} %iota_compare_fusion), kind=kLoop, calls=%fused_computation | loop fusion | flops 524288 | bytes 2162720 | tf_op jit(solution)/shard_map/add | solution.py:400
  (1 shorter events, 0.0 us)

commit v3 on v2

--- a/solution.py
+++ b/solution.py
@@ -218,6 +218,9 @@
 
         @pl.when(has_next)
         def _():
+            if i == 1:
+                moves[0].wait_send()
+                moves[2].wait_send()
             moves[i].start()
 
     def settle(i, out):
@@ -365,8 +368,7 @@
 
     @pl.when(has_next)
     def _():
-        for i in order:
-            moves[i].wait_send()
+        moves[1].wait_send()
 
 
 def local(old_ids, field_old, source_old, kappa_old, refine, neighbors, coarse_inverse):

time: 72.5 us -> 73 us (level)
  no operation moved by 1% of the time
where the time goes in v3:
time: 73 us; the launch traced here: 72.8 us
  Pallas kernels  70.3 us (96%)
  other arithmetic  2.46 us (3%)
    pallas_call x1, Pallas kernels, local(): pl.pallas_call(functools.partial(main_kernel, members, devices), out_shap...  70.3 us
    add x1, other arithmetic, local(): return u + jnp.where(half, low[:, None, :], high[:, None, :])  2.46 us

profile of v3, /device:TPU:0, one launch (start us, length us, event | category | flops | bytes accessed | tf_op | source)
XLA Modules:
  0.0 72.8 jit_solution(7714342482239621636)
XLA Ops:
  0.0 70.3 %shard_map.73 = (f32[8,32,1024]{2,1,0:T(8,128)}, f32[8,1024]{1,0:T(8,128)}, f32[8,1024]{1,0:T(8,128)}) custom-call(s32[16]{0:T(128)} %old_ids.1, s32[8,6]{1,0:T(8,128)} %nbrs.1, s32[8]{0:T(128)} %refine.1, f32[1,64,512]{2,1,0:T(8,128)} %inverse.1, f32[16,32,1024]{2,1,0:T(8,128)} %u_old.1, f32[16,32,1024]{2,1,0:T(8,128)} %f_old.1, f32[16,32,1024]{2,1,0:T(8,128)} %k_old.1), custom_call_target="tpu_custom_call" | custom-call | tf_op jit(solution)/shard_map/pallas_call | solution.py:387
  70.3 2.5 %select_add_fusion = f32[8,32,1024]{2,1,0:T(8,128)} fusion(f32[8,32,1024]{2,1,0:T(8,128)} %get-tuple-element.8, f32[8,1024]{1,0:T(8,128)} %get-tuple-element.10, f32[8,1024]{1,0:T(8,128)} %get-tuple-element.9, pred[32]{0:T(512)(128)(4,1)S(1)} %iota_compare_fusion), kind=kLoop, calls=%fused_computation | loop fusion | flops 524288 | bytes 2162720 | tf_op jit(solution)/shard_map/add | solution.py:402
  (1 shorter events, 0.0 us)

commit v4 on v2

--- a/solution.py
+++ b/solution.py
@@ -280,7 +280,6 @@
         return carry
 
     lax.fori_loop(0, NB, weigh, 0)
-    settle(1, f_ref)
 
     def terms(b, part, with_diagonal):
         rows = slice(8 * part, 8 * part + 8)
@@ -292,24 +291,48 @@
             applied = applied + weight * (u - around[face])
             if with_diagonal:
                 diagonal = diagonal + weight
-        return u, f_ref[b, rows, :] - applied, diagonal
+        return u, applied, diagonal
 
     def sweep(b, carry):
         for part in range(4):
-            u, gap, diagonal = terms(b, part, True)
-            u_ref[b, 8 * part : 8 * part + 8, :] = u + OMEGA * gap / diagonal
+            rows = slice(8 * part, 8 * part + 8)
+            u, applied, diagonal = terms(b, part, True)
+            u_ref[b, rows, :] = u + OMEGA * (f_ref[b, rows, :] - applied) / diagonal
         return carry
 
+    gain = gots[0]
+
+    def early(b, carry):
+        for part in range(4):
+            rows = slice(8 * part, 8 * part + 8)
+            u, applied, diagonal = terms(b, part, True)
+            factor = OMEGA / diagonal
+            gain[b, rows, :] = factor
+            u_ref[b, rows, :] = u - factor * applied
+        return carry
+
+    def late(b, carry):
+        u_ref[b] = u_ref[b] + gain[b] * f_ref[b]
+        return carry
+
+    lax.fori_loop(0, NB, early, 0)
+    settle(1, f_ref)
+    lax.fori_loop(0, NB, late, 0)
+
     for phase in (1, 2):
-        lax.fori_loop(0, NB, sweep, 0)
+        if phase == 2:
+            lax.fori_loop(0, NB, sweep, 0)
         send_faces(phase, u_ref)
         take_faces(phase)
         fill(u_ref, ghost[phase], nbrs, pad_u, sheet_u, False)
 
     def residual(b, carry):
         for half in (0, 1):
-            gap = terms(b, 2 * half, False)[1] + terms(b, 2 * half + 1, False)[1]
-            sums[2 * b + half] = gap
+            gap = [
+                f_ref[b, 8 * part : 8 * part + 8, :] - terms(b, part, False)[1]
+                for part in (2 * half, 2 * half + 1)
+            ]
+            sums[2 * b + half] = gap[0] + gap[1]
         return carry
 
     lax.fori_loop(0, NB, residual, 0)

time: 72.5 us -> 72.6 us (level)
  no operation moved by 1% of the time
where the time goes in v4:
time: 72.6 us; the launch traced here: 72.4 us
  Pallas kernels  70 us (96%)
  other arithmetic  2.46 us (3%)
    pallas_call x1, Pallas kernels, local(): pl.pallas_call(functools.partial(main_kernel, members, devices), out_shap...  70 us
    add x1, other arithmetic, local(): return u + jnp.where(half, low[:, None, :], high[:, None, :])  2.46 us

profile of v4, /device:TPU:0, one launch (start us, length us, event | category | flops | bytes accessed | tf_op | source)
XLA Modules:
  0.0 72.4 jit_solution(4991254144726369224)
XLA Ops:
  0.0 70.0 %shard_map.73 = (f32[8,32,1024]{2,1,0:T(8,128)}, f32[8,1024]{1,0:T(8,128)}, f32[8,1024]{1,0:T(8,128)}) custom-call(s32[16]{0:T(128)} %old_ids.1, s32[8,6]{1,0:T(8,128)} %nbrs.1, s32[8]{0:T(128)} %refine.1, f32[1,64,512]{2,1,0:T(8,128)} %inverse.1, f32[16,32,1024]{2,1,0:T(8,128)} %u_old.1, f32[16,32,1024]{2,1,0:T(8,128)} %f_old.1, f32[16,32,1024]{2,1,0:T(8,128)} %k_old.1), custom_call_target="tpu_custom_call" | custom-call | tf_op jit(solution)/shard_map/pallas_call | solution.py:408
  70.0 2.5 %select_add_fusion = f32[8,32,1024]{2,1,0:T(8,128)} fusion(f32[8,32,1024]{2,1,0:T(8,128)} %get-tuple-element.8, f32[8,1024]{1,0:T(8,128)} %get-tuple-element.10, f32[8,1024]{1,0:T(8,128)} %get-tuple-element.9, pred[32]{0:T(512)(128)(4,1)S(1)} %iota_compare_fusion), kind=kLoop, calls=%fused_computation | loop fusion | flops 524288 | bytes 2162720 | tf_op jit(solution)/shard_map/add | solution.py:423
  (1 shorter events, 0.0 us)
